TPU v7x, 256 devices: a whole 4x4x8 slice. The times are simulated.
256 devices in a mesh: az: 16 (over z, x_hi), rad: 2 (over core), ax: 8 (over y, x_lo).
Axes of the slice: x: 4 (x_hi: 2, x_lo: 2; x = x_hi * 2 + x_lo), y: 4, z: 8, core: 2. Of those that a mesh axis runs over, the one named last changes fastest.
Arguments:
- velocity: float32 [3, 128, 128, 1024], P(None, 'az', 'rad', 'ax'), may hold values from -6 to 6
- strain_rate: float32 [6, 128, 128, 1024], P(None, 'az', 'rad', 'ax'), may hold values from -6 to 6
- lm_average: float32 [128, 128, 1024], P('az', 'rad', 'ax'), may hold values from -8 to 8
- mm_average: float32 [128, 128, 1024], P('az', 'rad', 'ax'), may hold values from 1 to 20
- source_owner: int32 [128, 128, 8], P('az', 'rad', 'ax'), may hold values from 0 to 255, as said below
- source_block: int32 [128, 128, 8], P('az', 'rad', 'ax'), may hold values from 0 to 511
- offset_cells: int32 [128, 128, 8], P('az', 'rad', 'ax'), may hold values from 0 to 7
- fraction: float32 [128, 128, 8], P('az', 'rad', 'ax'), may hold values from 0 to 1
- query_count: int32 [256], replicated, may hold values from 64 to 512, as said below
Outputs:
- lm_updated: float32 [128, 128, 1024], P('az', 'rad', 'ax')
- mm_updated: float32 [128, 128, 1024], P('az', 'rad', 'ax')
- eddy_viscosity: float32 [128, 128, 1024], P('az', 'rad', 'ax')
Inputs may be any that keep to these rules, and one draw needn't show every extreme that they name: `source_owner`: each block's source owner is the querying device itself, the device one az index lower or higher (around the loop of az), or the device whose rad index differs in the lowest bit; it has the querying device's ax index. Among the live blocks of one device at most 128 name any one owner, and a device with all 512 blocks live names each of the four exactly 128 times. `query_count`: some device has all 512 blocks live.
All inputs are finite; a program needn't handle non-finite values.
Results may differ from a plain program's by a relative error of at most 0.0012.
Values sent between devices are 32-bit elements; how exact they have to be, the bound alone decides.
A program may use at most 128 MiB of HBM per device.

v0:
```python
import jax
import jax.numpy as jnp
from jax import lax
from jax.sharding import PartitionSpec as P

pair_list = ((0, 0), (1, 1), (2, 2), (0, 1), (0, 2), (1, 2))
delta_sq = 0.25
relax_rate = 0.5


def extended(cells, sides, width, closed):
    for axis, dim in sides:
        count = lax.axis_size(axis)
        ends = count if closed else count - 1
        head = lax.slice_in_dim(cells, 0, width, axis=dim)
        tail = lax.slice_in_dim(cells, cells.shape[dim] - width, cells.shape[dim], axis=dim)
        cells = jnp.concatenate(
            [
                lax.ppermute(tail, axis, [(i, (i + 1) % count) for i in range(ends)]),
                cells,
                lax.ppermute(head, axis, [((i + 1) % count, i) for i in range(ends)]),
            ],
            axis=dim,
        )
    return cells


def shifted_2(value, axis, by):
    length = lax.axis_size(axis)
    return lax.ppermute(value, axis, [(i, (i + by) % length) for i in range(length)])


def from_partner(value, axis, apart):
    mask = 2**apart
    pairs = [(source, source ^ mask) for source in range(lax.axis_size(axis))]
    return lax.ppermute(value, axis, pairs)


def strain_norm(strain):
    normal = strain[0] * strain[0] + strain[1] * strain[1] + strain[2] * strain[2]
    shearing = strain[3] * strain[3] + strain[4] * strain[4] + strain[5] * strain[5]
    return jnp.sqrt(2.0 * normal + 4.0 * shearing)


def products(velocity, strain, magnitude):
    fields = [velocity[0], velocity[1], velocity[2]]
    fields += [velocity[left_comp] * velocity[right_comp] for left_comp, right_comp in pair_list]
    fields += [strain[channel] for channel in range(6)]
    fields += [magnitude * strain[channel] for channel in range(6)]
    return fields


def contract(filtered):
    magnitude = strain_norm([filtered[9 + channel] for channel in range(6)])
    lm_sum = 0.0
    mm_sum = 0.0
    for channel, (left_comp, right_comp) in enumerate(pair_list):
        weight = 1.0 if channel < 3 else 2.0
        leonard = filtered[3 + channel] - filtered[left_comp] * filtered[right_comp]
        model_term = (
            2.0 * delta_sq * (filtered[15 + channel] - 4.0 * magnitude * filtered[9 + channel])
        )
        lm_sum = lm_sum + weight * leonard * model_term
        mm_sum = mm_sum + weight * model_term * model_term
    return (lm_sum, mm_sum)


def smooth(values, axis_dim):
    interior = values.shape[axis_dim] - 2
    before = lax.slice_in_dim(values, 0, interior, axis=axis_dim)
    middle = lax.slice_in_dim(values, 1, interior + 1, axis=axis_dim)
    behind = lax.slice_in_dim(values, 2, interior + 2, axis=axis_dim)
    return 0.25 * before + 0.5 * middle + 0.25 * behind


def interpolate(line_values, offsets, fraction):
    padded = jnp.concatenate(
        [
            jnp.broadcast_to(line_values[..., :1], line_values.shape[:-1] + (7,)),
            line_values,
            line_values[..., 127:],
        ],
        axis=-1,
    )
    weight = fraction[None, :, None]
    total = jnp.zeros(line_values.shape, jnp.float32)
    for step_back in range(-1, 8):
        shifted = padded[..., 7 - step_back : 135 - step_back]
        left_hit = (offsets == step_back)[None, :, None]
        right_hit = (offsets - 1 == step_back)[None, :, None]
        factor = jnp.where(left_hit, 1.0 - weight, 0.0) + jnp.where(right_hit, weight, 0.0)
        total = total + factor * shifted
    return total


def relax(lm_here, mm_here, upstream_lm, upstream_mm, magnitude):
    rate_ratio = relax_rate * jnp.power(jnp.maximum(upstream_lm, 0.0) * upstream_mm, 0.125)
    weight = rate_ratio / (1.0 + rate_ratio)
    lm_new = jnp.maximum(weight * lm_here + (1.0 - weight) * upstream_lm, 0.0)
    mm_new = weight * mm_here + (1.0 - weight) * upstream_mm
    return (lm_new, mm_new, delta_sq * lm_new / mm_new * magnitude)


def select_lines(block_table, line_ids):
    selector = (
        line_ids[:, None] == jnp.arange(block_table.shape[1], dtype=jnp.int32)[None, :]
    ).astype(jnp.float32)
    return jnp.einsum(
        "gp,ops->ogs",
        selector,
        block_table,
        precision=lax.Precision.HIGHEST,
        preferred_element_type=jnp.float32,
    )


def on_device(
    velocity,
    strain_rate,
    lm_average,
    mm_average,
    source_owner,
    source_block,
    offset_cells,
    fraction,
    query_count,
):
    magnitude = strain_norm(strain_rate)
    stacked = jnp.stack(products(velocity, strain_rate, magnitude))
    filtered = smooth(extended(stacked, (("az", 1),), 1, True), 1)
    filtered = smooth(extended(filtered, (("rad", 2),), 1, False), 2)
    filtered = smooth(extended(filtered, (("ax", 3),), 1, False), 3)
    lm_here, mm_here = contract(filtered)
    extent = lm_average.shape
    line_count = extent[0] * extent[1] * (extent[2] // 128)
    block_table = jnp.stack([lm_average, mm_average]).reshape(2, line_count, 128)
    owner_id = source_owner.reshape(line_count)
    wanted = source_block.reshape(line_count)
    count_az = lax.axis_size("az")
    count_rad = lax.axis_size("rad")
    count_ax = lax.axis_size("ax")
    index_az = lax.axis_index("az")
    index_rad = lax.axis_index("rad")
    index_ax = lax.axis_index("ax")
    self_index = index_az * (count_rad * count_ax) + index_rad * count_ax + index_ax
    lower_peer = (
        jnp.remainder(index_az - 1, count_az) * (count_rad * count_ax)
        + index_rad * count_ax
        + index_ax
    )
    upper_peer = (
        jnp.remainder(index_az + 1, count_az) * (count_rad * count_ax)
        + index_rad * count_ax
        + index_ax
    )
    radial_peer = index_az * (count_rad * count_ax) + (1 - index_rad) * count_ax + index_ax
    direction = jnp.where(
        owner_id == lower_peer,
        1,
        jnp.where(owner_id == upper_peer, 2, jnp.where(owner_id == radial_peer, 3, 0)),
    ).astype(jnp.int32)
    device_hit = jnp.arange(query_count.shape[0], dtype=jnp.int32) == self_index
    live_count = jnp.sum(jnp.where(device_hit, query_count, 0))
    active = jnp.arange(line_count, dtype=jnp.int32) < live_count
    slot_hot = (
        (direction[:, None] == jnp.arange(4, dtype=jnp.int32)[None, :]) & active[:, None]
    ).astype(jnp.int32)
    line_order = jnp.arange(line_count, dtype=jnp.int32)
    lower_tri = (line_order[:, None] >= line_order[None, :]).astype(jnp.int32)
    slot_rank = jnp.dot(lower_tri, slot_hot, preferred_element_type=jnp.int32) - 1
    slot_index = jnp.sum(slot_rank * slot_hot, axis=1)
    capacity = line_count // 4
    target = jnp.where(active, direction * capacity + slot_index, 4 * capacity)
    slot_order = jnp.arange(4 * capacity, dtype=jnp.int32)
    asked = jnp.sum(
        jnp.where(slot_order[:, None] == target[None, :], wanted[None, :], 0), axis=1
    ).reshape(4, capacity)
    replies = [select_lines(block_table, asked[0])]
    for peer_row, shift_by in ((1, -1), (2, 1)):
        incoming = shifted_2(asked[peer_row], "az", shift_by)
        replies.append(shifted_2(select_lines(block_table, incoming), "az", -shift_by))
    incoming_radial = from_partner(asked[3], "rad", 0)
    replies.append(from_partner(select_lines(block_table, incoming_radial), "rad", 0))
    picked = select_lines(jnp.concatenate(replies, axis=1), jnp.minimum(target, 4 * capacity - 1))
    line_values = jnp.where(active[None, :, None], picked, block_table)
    upstream = interpolate(
        line_values, offset_cells.reshape(line_count), fraction.reshape(line_count)
    )
    upstream = upstream.reshape(2, extent[0], extent[1], extent[2])
    lm_new, mm_new, eddy = relax(lm_here, mm_here, upstream[0], upstream[1], magnitude)
    return (lm_new, mm_new, eddy)


def solution(mesh):
    placed = (
        P(None, "az", "rad", "ax"),
        P(None, "az", "rad", "ax"),
        P("az", "rad", "ax"),
        P("az", "rad", "ax"),
        P("az", "rad", "ax"),
        P("az", "rad", "ax"),
        P("az", "rad", "ax"),
        P("az", "rad", "ax"),
        P(),
    )
    return jax.shard_map(
        on_device,
        mesh=mesh,
        in_specs=placed,
        out_specs=(P("az", "rad", "ax"), P("az", "rad", "ax"), P("az", "rad", "ax")),
        check_vma=False,
    )
```

profile of v0, /device:TPU:103, one launch (start us, length us, event | category | flops | bytes accessed | tf_op | source)
XLA Modules:
  0.0 116.0 jit_solution(12108616449676434292)
XLA Ops:
  0.6 1.3 %constant_dynamic-update-slice_fusion.1 = f32[21,8,64,128]{3,2,1,0:T(8,128)S(1)} fusion(f32[3,8,64,128]{3,2,1,0:T(8,128)} %param.9), kind=kLoop, calls=%fused_computation.165 | loop fusion | bytes 1572864
  8.7 2.4 %copy-done.2 = f32[21,8,64,128]{3,2,1,0:T(8,128)} copy-done((f32[21,8,64,128]{3,2,1,0:T(8,128)}, f32[21,8,64,128]{3,2,1,0:T(8,128)S(1)}, u32[]{:S(2)}) %copy-start.2) | copy-done | bytes 5505048
  11.2 3.8 %collective-permute-start.6 = (f32[21,1,64,128]{3,2,1,0:T(8,128)S(1)}, f32[21,1,64,128]{3,2,1,0:T(8,128)S(1)}, u32[]{:S(2)}, u32[]{:S(2)}) collective-permute-start(f32[21,1,64,128]{3,2,1,0:T(8,128)S(1)} %get-tuple-element.23), channel_id=1, source_target_pairs={{0,16},{16,32},{32,48},{48,64},{64,80},{80,96},{96,112},{112,128},... | collective-permute-start | bytes 2064392 | tf_op jit(solution)/shard_map/ppermute | solution.py:19
  15.1 1.3 %fusion.116 = s32[]{:T(128)} fusion(s32[256]{0:T(256)} %param.17, s32[]{:T(128)S(6)} %add.298), kind=kLoop, calls=%fused_computation.215 | loop fusion | flops 767 | bytes 1032 | tf_op jit(solution)/shard_map/reduce_sum | solution.py:163
  21.1 1.3 %collective-permute-start = (s32[128]{0:T(128)}, s32[128]{0:T(128)}, u32[]{:S(2)}, u32[]{:S(2)}) collective-permute-start(s32[128]{0:T(128)} %get-tuple-element.32), channel_id=1, source_target_pairs={{0,240},{16,0},{32,16},{48,32},{64,48},{80,64},{96,80},{112,96},{1... | collective-permute-start | bytes 1544 | tf_op jit(solution)/shard_map/ppermute | solution.py:30
  22.4 3.8 %collective-permute-start.2 = (s32[128]{0:T(128)}, s32[128]{0:T(128)}, u32[]{:S(2)}, u32[]{:S(2)}) collective-permute-start(s32[128]{0:T(128)} %get-tuple-element.31), channel_id=1, source_target_pairs={{0,16},{16,32},{32,48},{48,64},{64,80},{80,96},{96,112},{112,128},... | collective-permute-start | bytes 1544 | tf_op jit(solution)/shard_map/ppermute | solution.py:30
  26.2 1.5 %collective-permute-start.4 = (s32[128]{0:T(128)}, s32[128]{0:T(128)}, u32[]{:S(2)}, u32[]{:S(2)}) collective-permute-start(s32[128]{0:T(128)} %get-tuple-element.30), channel_id=1, source_target_pairs={{0,8},{8,0},{1,9},{9,1},{2,10},{10,2},{3,11},{11,3},{4,12},{12,4},... | collective-permute-start | bytes 1544 | tf_op jit(solution)/shard_map/ppermute | solution.py:36
  27.7 1.4 %fusion.115 = (f32[8,64]{1,0:T(8,128)}, f32[8,64]{1,0:T(8,128)S(1)}, f32[8,64]{1,0:T(8,128)}, f32[8,64]{1,0:T(8,128)}, f32[8,64]{1,0:T(8,128)}, /*index=5*/f32[8...) fusion(f32[8,64,1]{1,2,0:T(1,128)} %param.16, s32[8,64,1]{1,2,0:T(1,128)} %param.15), kind=kLoop, calls=%fused_computation.209 | loop fusion | flops 24064 | bytes 22528 | tf_op jit(solution)/shard_map/add | solution.py:91
  29.2 1.3 %reshape.421 = f32[512]{0:T(512)} reshape(f32[8,64]{1,0:T(8,128)} %get-tuple-element.3) | data formatting | bytes 4096 | tf_op jit(solution)/shard_map/add | solution.py:91
  30.5 1.3 %reshape.422 = f32[512]{0:T(512)} reshape(f32[8,64]{1,0:T(8,128)} %get-tuple-element.8) | data formatting | bytes 4096 | tf_op jit(solution)/shard_map/add | solution.py:91
  31.8 1.3 %reshape.423 = f32[512]{0:T(512)} reshape(f32[8,64]{1,0:T(8,128)} %get-tuple-element.7) | data formatting | bytes 4096 | tf_op jit(solution)/shard_map/add | solution.py:91
  33.2 1.4 %reshape.424 = f32[512]{0:T(512)} reshape(f32[8,64]{1,0:T(8,128)} %get-tuple-element.6) | data formatting | bytes 4096 | tf_op jit(solution)/shard_map/add | solution.py:91
  34.5 1.3 %reshape.425 = f32[512]{0:T(512)} reshape(f32[8,64]{1,0:T(8,128)} %get-tuple-element.5) | data formatting | bytes 4096 | tf_op jit(solution)/shard_map/add | solution.py:91
  36.8 6.5 %collective-permute-done = s32[128]{0:T(128)} collective-permute-done((s32[128]{0:T(128)}, s32[128]{0:T(128)}, u32[]{:S(2)}, u32[]{:S(2)}) %collective-permute-start) | collective-permute-done | bytes 544 | tf_op jit(solution)/shard_map/ppermute | solution.py:30
  44.3 6.9 %collective-permute-start.1 = (f32[2,128,128]{2,1,0:T(8,128)S(1)}, f32[2,128,128]{2,1,0:T(8,128)S(1)}, u32[]{:S(2)}, u32[]{:S(2)}) collective-permute-start(f32[2,128,128]{2,1,0:T(8,128)S(1)} %convolution_bitcast_fusion.3), channel_id=1, source_target_pairs={{0,16},{16,32},{32,48},{48,64},{64,80},{80,96},{96,112},{112,128},... | collective-permute-start | bytes 393224 | tf_op jit(solution)/shard_map/ppermute | solution.py:30
  53.3 1.4 %collective-permute-start.5 = (f32[2,128,128]{2,1,0:T(8,128)S(1)}, f32[2,128,128]{2,1,0:T(8,128)S(1)}, u32[]{:S(2)}, u32[]{:S(2)}) collective-permute-start(f32[2,128,128]{2,1,0:T(8,128)S(1)} %convolution_bitcast_fusion.1), channel_id=1, source_target_pairs={{0,8},{8,0},{1,9},{9,1},{2,10},{10,2},{3,11},{11,3},{4,12},{12,4},... | collective-permute-start | bytes 393224 | tf_op jit(solution)/shard_map/ppermute | solution.py:36
  55.7 4.0 %collective-permute-done.3 = f32[2,128,128]{2,1,0:T(8,128)S(1)} collective-permute-done((f32[2,128,128]{2,1,0:T(8,128)S(1)}, f32[2,128,128]{2,1,0:T(8,128)S(1)}, u32[]{:S(2)}, u32[]{:S(2)}) %collective-permute-start.3) | collective-permute-done | bytes 131104 | tf_op jit(solution)/shard_map/ppermute | solution.py:30
  59.7 1.4 %fusion.12 = f32[2,512,128]{2,1,0:T(8,128)S(1)} fusion(f32[2,128,128]{2,1,0:T(8,128)S(1)} %collective-permute-done.5, f32[2,128,128]{2,1,0:T(8,128)S(1)} %collective-permute-done.3, f32[2,128,128]{2,1,0:T(8,128)S(1)} %collective-permute-done.1, f32[2,128,128]{2,1,0:T(8,128)S(1)} %convolution_bitcast_fusion.4, s32[512]{0:T(512)} %get-tuple-element.15, ...), kind=kOutput, calls=%fused_computation.31 | convolution fusion | flops 806223872 | bytes 1575424 | tf_op jit(solution)/shard_map/gp,ops->ogs/dot_general | solution.py:108
  61.5 2.6 %fusion.9 = f32[21,8,64,128]{3,2,1,0:T(8,128)S(1)} fusion(f32[21,1,64,128]{3,2,1,0:T(8,128)S(1)} %collective-permute-done.7, f32[21,8,64,128]{3,2,1,0:T(8,128)S(1)} %copy-done.3, f32[21,1,64,128]{3,2,1,0:T(8,128)S(1)} %collective-permute-done.6), kind=kLoop, calls=%fused_computation.14 | loop fusion | flops 9633792 | bytes 12386304 | tf_op jit(solution)/shard_map/add | solution.py:73
  64.3 1.3 %collective-permute-start.8 = (f32[21,8,1,128]{3,2,1,0:T(1,128)S(1)}, f32[21,8,1,128]{3,2,1,0:T(1,128)S(1)}, u32[]{:S(2)}, u32[]{:S(2)}) collective-permute-start(f32[21,8,1,128]{3,2,1,0:T(1,128)S(1)} %get-tuple-element.21), channel_id=1, source_target_pairs={{0,8},{1,9},{2,10},{3,11},{4,12},{5,13},{6,14},{7,15},{16,24},{17,... | collective-permute-start | bytes 258056 | tf_op jit(solution)/shard_map/ppermute | solution.py:19
  65.6 4.5 %collective-permute-start.9 = (f32[21,8,1,128]{3,2,1,0:T(1,128)S(1)}, f32[21,8,1,128]{3,2,1,0:T(1,128)S(1)}, u32[]{:S(2)}, u32[]{:S(2)}) collective-permute-start(f32[21,8,1,128]{3,2,1,0:T(1,128)S(1)} %get-tuple-element.22), channel_id=1, source_target_pairs={{8,0},{9,1},{10,2},{11,3},{12,4},{13,5},{14,6},{15,7},{24,16},{25,... | collective-permute-start | bytes 258056 | tf_op jit(solution)/shard_map/ppermute | solution.py:21
  70.3 2.8 %fusion.20 = f32[2,512,128]{2,1,0:T(8,128)S(1)} fusion(f32[2,512,128]{2,1,0:T(8,128)S(1)} %fusion.12, f32[2,512,7]{2,1,0:T(8,128)S(1)} %broadcast_in_dim.117, f32[2,512,1]{2,1,0:T(8,128)S(1)} %get-tuple-element.27, f32[512]{0:T(512)S(1)} %reshape.429, f32[512]{0:T(512)S(1)} %reshape.428, f32[512]{0:T(512)S(1)} %reshape.427, f32[512]{0:T(512)S(1)} %copy-done.11, ...), kind=kLoop, calls=%fused_computation.47 | loop fusion | flops 3276800 | bytes 1099776 | tf_op jit(solution)/shard_map/add | solution.py:92
  73.2 2.5 %fusion.5 = f32[21,8,64,128]{3,2,1,0:T(8,128)S(1)} fusion(f32[21,8,1,128]{3,2,1,0:T(1,128)S(1)} %collective-permute-done.9, f32[21,8,64,128]{3,2,1,0:T(8,128)S(1)} %fusion.9, f32[21,8,1,128]{3,2,1,0:T(1,128)S(1)} %collective-permute-done.8), kind=kLoop, calls=%fused_computation.8 | loop fusion | flops 9633792 | bytes 11182080 | tf_op jit(solution)/shard_map/add | solution.py:73
  75.8 6.2 %fusion.124 = (f32[21,8,64,1]{3,2,1,0:T(8,128)}, f32[21,8,64,1]{3,2,1,0:T(8,128)}) fusion(f32[21,8,64,128]{3,2,1,0:T(8,128)S(1)} %fusion.5), kind=kLoop, calls=%fused_computation.222 | loop fusion | bytes 172032 | tf_op jit(solution)/shard_map/slice | solution.py:16
  82.0 3.7 %copy.54 = f32[21,8,64,1]{2,1,3,0:T(8,128)S(1)} copy(f32[21,8,64,1]{3,2,1,0:T(8,128)} %get-tuple-element.19) | data formatting | bytes 86016 | tf_op jit(solution)/shard_map/slice | solution.py:16
  85.7 2.8 %collective-permute-start.10 = (f32[21,8,64,1]{2,1,3,0:T(8,128)S(1)}, f32[21,8,64,1]{2,1,3,0:T(8,128)S(1)}, u32[]{:S(2)}, u32[]{:S(2)}) collective-permute-start(f32[21,8,64,1]{2,1,3,0:T(8,128)S(1)} %copy.54), channel_id=1, source_target_pairs={{0,1},{1,2},{2,3},{3,4},{4,5},{5,6},{6,7},{8,9},{9,10},{10,11},{11... | collective-permute-start | bytes 129032 | tf_op jit(solution)/shard_map/ppermute | solution.py:19
  88.6 3.7 %copy.56 = f32[21,8,64,1]{2,1,3,0:T(8,128)S(1)} copy(f32[21,8,64,1]{3,2,1,0:T(8,128)} %get-tuple-element.20) | data formatting | bytes 86016 | tf_op jit(solution)/shard_map/slice | solution.py:15
  92.3 2.4 %collective-permute-start.11 = (f32[21,8,64,1]{2,1,3,0:T(8,128)S(1)}, f32[21,8,64,1]{2,1,3,0:T(8,128)S(1)}, u32[]{:S(2)}, u32[]{:S(2)}) collective-permute-start(f32[21,8,64,1]{2,1,3,0:T(8,128)S(1)} %copy.56), channel_id=1, source_target_pairs={{1,0},{2,1},{3,2},{4,3},{5,4},{6,5},{7,6},{9,8},{10,9},{11,10},{12... | collective-permute-start | bytes 129032 | tf_op jit(solution)/shard_map/ppermute | solution.py:21
  94.8 3.4 %copy.55 = f32[21,8,64,1]{3,2,1,0:T(8,128)} copy(f32[21,8,64,1]{2,1,3,0:T(8,128)S(1)} %collective-permute-done.10) | data formatting | bytes 86016 | tf_op jit(solution)/shard_map/ppermute | solution.py:19
  99.5 3.4 %copy.57 = f32[21,8,64,1]{3,2,1,0:T(8,128)} copy(f32[21,8,64,1]{2,1,3,0:T(8,128)S(1)} %collective-permute-done.11) | data formatting | bytes 86016 | tf_op jit(solution)/shard_map/ppermute | solution.py:21
  103.0 11.1 %fusion.1 = f32[21,8,64,128]{3,2,1,0:T(8,128)S(1)} fusion(f32[21,8,64,1]{3,2,1,0:T(8,128)} %copy.57, f32[21,8,64,128]{3,2,1,0:T(8,128)} %copy-done, f32[21,8,64,1]{3,2,1,0:T(8,128)} %copy.55), kind=kLoop, calls=%fused_computation.2 | loop fusion | flops 9633792 | bytes 11096064 | tf_op jit(solution)/shard_map/add | solution.py:73
  114.1 1.9 %bitcast_multiply_fusion = (f32[8,64,128]{2,1,0:T(8,128)}, f32[8,64,128]{2,1,0:T(8,128)}, f32[8,64,128]{2,1,0:T(8,128)}) fusion(f32[1,8,64,128]{3,2,1,0:T(8,128)S(1)} %get-tuple-element.18, f32[8,64,128]{2,1,0:T(8,128)S(1)} %bitcast.223, f32[21,8,64,128]{3,2,1,0:T(8,128)S(1)} %fusion.1, f32[8,64,128]{2,1,0:T(8,128)S(1)} %bitcast.222), kind=kLoop, calls=%fused_computation.137 | loop fusion | flops 5570560 | bytes 7077888 | tf_op jit(solution)/shard_map/mul | solution.py:101
  (77 shorter events, 18.5 us)
Async XLA Ops:
  0.6 7.4 %copy-start.1 = (f32[6,8,64,128]{3,2,1,0:T(8,128)S(1)}, f32[6,8,64,128]{3,2,1,0:T(8,128)}, u32[]{:S(2)}) copy-start(f32[6,8,64,128]{3,2,1,0:T(8,128)} %param.10) | copy-start | bytes 4718596
  8.1 6.9 %copy-start.12 = (s32[8,64,1]{1,2,0:T(1,128)S(1)}, s32[8,64,1]{1,2,0:T(1,128)}, u32[]{:S(2)}) copy-start(s32[8,64,1]{1,2,0:T(1,128)} %param.13) | copy-start | bytes 6148
  8.1 11.5 %copy-start.13 = (s32[8,64,1]{1,2,0:T(1,128)S(1)}, s32[8,64,1]{1,2,0:T(1,128)}, u32[]{:S(2)}) copy-start(s32[8,64,1]{1,2,0:T(1,128)} %param.14) | copy-start | bytes 6148
  8.1 35.2 %copy-start.4 = (f32[8,64,128]{2,1,0:T(8,128)S(1)}, f32[8,64,128]{2,1,0:T(8,128)}, u32[]{:S(2)}) copy-start(f32[8,64,128]{2,1,0:T(8,128)} %param.12) | copy-start | bytes 786436
  8.1 35.2 %copy-start.5 = (f32[8,64,128]{2,1,0:T(8,128)S(1)}, f32[8,64,128]{2,1,0:T(8,128)}, u32[]{:S(2)}) copy-start(f32[8,64,128]{2,1,0:T(8,128)} %param.11) | copy-start | bytes 786436
  8.7 2.4 %copy-start.2 = (f32[21,8,64,128]{3,2,1,0:T(8,128)}, f32[21,8,64,128]{3,2,1,0:T(8,128)S(1)}, u32[]{:S(2)}) copy-start(f32[21,8,64,128]{3,2,1,0:T(8,128)S(1)} %multiply_dynamic-update-slice_fusion) | copy-start | bytes 16515076
  11.2 50.3 %collective-permute-start.6 = (f32[21,1,64,128]{3,2,1,0:T(8,128)S(1)}, f32[21,1,64,128]{3,2,1,0:T(8,128)S(1)}, u32[]{:S(2)}, u32[]{:S(2)}) collective-permute-start(f32[21,1,64,128]{3,2,1,0:T(8,128)S(1)} %get-tuple-element.23), channel_id=1, source_target_pairs={{0,16},{16,32},{32,48},{48,64},{64,80},{80,96},{96,112},{112,128},... | collective-permute-start | bytes 2064392 | tf_op jit(solution)/shard_map/ppermute | solution.py:19
  15.0 46.5 %collective-permute-start.7 = (f32[21,1,64,128]{3,2,1,0:T(8,128)S(1)}, f32[21,1,64,128]{3,2,1,0:T(8,128)S(1)}, u32[]{:S(2)}, u32[]{:S(2)}) collective-permute-start(f32[21,1,64,128]{3,2,1,0:T(8,128)S(1)} %get-tuple-element.24), channel_id=1, source_target_pairs={{16,0},{32,16},{48,32},{64,48},{80,64},{96,80},{112,96},{128,112},... | collective-permute-start | bytes 2064392 | tf_op jit(solution)/shard_map/ppermute | solution.py:21
  17.1 0.5 copy-start.14
  21.1 22.2 %collective-permute-start = (s32[128]{0:T(128)}, s32[128]{0:T(128)}, u32[]{:S(2)}, u32[]{:S(2)}) collective-permute-start(s32[128]{0:T(128)} %get-tuple-element.32), channel_id=1, source_target_pairs={{0,240},{16,0},{32,16},{48,32},{64,48},{80,64},{96,80},{112,96},{1... | collective-permute-start | bytes 1544 | tf_op jit(solution)/shard_map/ppermute | solution.py:30
  22.4 28.8 %collective-permute-start.2 = (s32[128]{0:T(128)}, s32[128]{0:T(128)}, u32[]{:S(2)}, u32[]{:S(2)}) collective-permute-start(s32[128]{0:T(128)} %get-tuple-element.31), channel_id=1, source_target_pairs={{0,16},{16,32},{32,48},{48,64},{64,80},{80,96},{96,112},{112,128},... | collective-permute-start | bytes 1544 | tf_op jit(solution)/shard_map/ppermute | solution.py:30
  26.2 26.0 %collective-permute-start.4 = (s32[128]{0:T(128)}, s32[128]{0:T(128)}, u32[]{:S(2)}, u32[]{:S(2)}) collective-permute-start(s32[128]{0:T(128)} %get-tuple-element.30), channel_id=1, source_target_pairs={{0,8},{8,0},{1,9},{9,1},{2,10},{10,2},{3,11},{11,3},{4,12},{12,4},... | collective-permute-start | bytes 1544 | tf_op jit(solution)/shard_map/ppermute | solution.py:36
  36.8 24.8 %copy-start.3 = (f32[21,8,64,128]{3,2,1,0:T(8,128)S(1)}, f32[21,8,64,128]{3,2,1,0:T(8,128)}, u32[]{:S(2)}) copy-start(f32[21,8,64,128]{3,2,1,0:T(8,128)} %copy-done.2) | copy-start | bytes 16515076
  44.3 11.4 %collective-permute-start.1 = (f32[2,128,128]{2,1,0:T(8,128)S(1)}, f32[2,128,128]{2,1,0:T(8,128)S(1)}, u32[]{:S(2)}, u32[]{:S(2)}) collective-permute-start(f32[2,128,128]{2,1,0:T(8,128)S(1)} %convolution_bitcast_fusion.3), channel_id=1, source_target_pairs={{0,16},{16,32},{32,48},{48,64},{64,80},{80,96},{96,112},{112,128},... | collective-permute-start | bytes 393224 | tf_op jit(solution)/shard_map/ppermute | solution.py:30
  52.2 7.5 %collective-permute-start.3 = (f32[2,128,128]{2,1,0:T(8,128)S(1)}, f32[2,128,128]{2,1,0:T(8,128)S(1)}, u32[]{:S(2)}, u32[]{:S(2)}) collective-permute-start(f32[2,128,128]{2,1,0:T(8,128)S(1)} %convolution_bitcast_fusion.2), channel_id=1, source_target_pairs={{0,240},{16,0},{32,16},{48,32},{64,48},{80,64},{96,80},{112,96},{1... | collective-permute-start | bytes 393224 | tf_op jit(solution)/shard_map/ppermute | solution.py:30
  53.3 6.4 %collective-permute-start.5 = (f32[2,128,128]{2,1,0:T(8,128)S(1)}, f32[2,128,128]{2,1,0:T(8,128)S(1)}, u32[]{:S(2)}, u32[]{:S(2)}) collective-permute-start(f32[2,128,128]{2,1,0:T(8,128)S(1)} %convolution_bitcast_fusion.1), channel_id=1, source_target_pairs={{0,8},{8,0},{1,9},{9,1},{2,10},{10,2},{3,11},{11,3},{4,12},{12,4},... | collective-permute-start | bytes 393224 | tf_op jit(solution)/shard_map/ppermute | solution.py:36
  61.4 8.9 %copy-start.6 = (f32[512]{0:T(512)S(1)}, f32[512]{0:T(512)}, u32[]{:S(2)}) copy-start(f32[512]{0:T(512)} %reshape.421) | copy-start | bytes 6148
  61.4 8.9 %copy-start.7 = (f32[512]{0:T(512)S(1)}, f32[512]{0:T(512)}, u32[]{:S(2)}) copy-start(f32[512]{0:T(512)} %reshape.422) | copy-start | bytes 6148
  61.4 8.9 %copy-start.8 = (f32[512]{0:T(512)S(1)}, f32[512]{0:T(512)}, u32[]{:S(2)}) copy-start(f32[512]{0:T(512)} %reshape.423) | copy-start | bytes 6148
  61.5 8.9 %copy-start.9 = (f32[512]{0:T(512)S(1)}, f32[512]{0:T(512)}, u32[]{:S(2)}) copy-start(f32[512]{0:T(512)} %reshape.424) | copy-start | bytes 6148
  61.5 8.9 %copy-start.10 = (f32[512]{0:T(512)S(1)}, f32[512]{0:T(512)}, u32[]{:S(2)}) copy-start(f32[512]{0:T(512)} %reshape.425) | copy-start | bytes 6148
  61.5 8.9 %copy-start.11 = (f32[512]{0:T(512)S(1)}, f32[512]{0:T(512)}, u32[]{:S(2)}) copy-start(f32[512]{0:T(512)} %reshape.426) | copy-start | bytes 6148
  64.3 8.9 %collective-permute-start.8 = (f32[21,8,1,128]{3,2,1,0:T(1,128)S(1)}, f32[21,8,1,128]{3,2,1,0:T(1,128)S(1)}, u32[]{:S(2)}, u32[]{:S(2)}) collective-permute-start(f32[21,8,1,128]{3,2,1,0:T(1,128)S(1)} %get-tuple-element.21), channel_id=1, source_target_pairs={{0,8},{1,9},{2,10},{3,11},{4,12},{5,13},{6,14},{7,15},{16,24},{17,... | collective-permute-start | bytes 258056 | tf_op jit(solution)/shard_map/ppermute | solution.py:19
  65.6 7.6 %collective-permute-start.9 = (f32[21,8,1,128]{3,2,1,0:T(1,128)S(1)}, f32[21,8,1,128]{3,2,1,0:T(1,128)S(1)}, u32[]{:S(2)}, u32[]{:S(2)}) collective-permute-start(f32[21,8,1,128]{3,2,1,0:T(1,128)S(1)} %get-tuple-element.22), channel_id=1, source_target_pairs={{8,0},{9,1},{10,2},{11,3},{12,4},{13,5},{14,6},{15,7},{24,16},{25,... | collective-permute-start | bytes 258056 | tf_op jit(solution)/shard_map/ppermute | solution.py:21
  75.7 6.3 %copy-start = (f32[21,8,64,128]{3,2,1,0:T(8,128)}, f32[21,8,64,128]{3,2,1,0:T(8,128)S(1)}, u32[]{:S(2)}) copy-start(f32[21,8,64,128]{3,2,1,0:T(8,128)S(1)} %fusion.5) | copy-start | bytes 16515076
  85.7 9.1 %collective-permute-start.10 = (f32[21,8,64,1]{2,1,3,0:T(8,128)S(1)}, f32[21,8,64,1]{2,1,3,0:T(8,128)S(1)}, u32[]{:S(2)}, u32[]{:S(2)}) collective-permute-start(f32[21,8,64,1]{2,1,3,0:T(8,128)S(1)} %copy.54), channel_id=1, source_target_pairs={{0,1},{1,2},{2,3},{3,4},{4,5},{5,6},{6,7},{8,9},{9,10},{10,11},{11... | collective-permute-start | bytes 129032 | tf_op jit(solution)/shard_map/ppermute | solution.py:19
  92.3 7.2 %collective-permute-start.11 = (f32[21,8,64,1]{2,1,3,0:T(8,128)S(1)}, f32[21,8,64,1]{2,1,3,0:T(8,128)S(1)}, u32[]{:S(2)}, u32[]{:S(2)}) collective-permute-start(f32[21,8,64,1]{2,1,3,0:T(8,128)S(1)} %copy.56), channel_id=1, source_target_pairs={{1,0},{2,1},{3,2},{4,3},{5,4},{6,5},{7,6},{9,8},{10,9},{11,10},{12... | collective-permute-start | bytes 129032 | tf_op jit(solution)/shard_map/ppermute | solution.py:21
where the time goes:
time: 117 us; the launch traced here: 116 us
  local copies, waits for them, and re-layouts  34.7 us (30%)
  other arithmetic  33 us (28%)
  starting transfers between devices  29.8 us (25%)
  waiting for transfers between devices  11.8 us (10%)
  matrix products  5.59 us (5%)
    add x3, other arithmetic, smooth(): return 0.25 * before + 0.5 * middle + 0.25 * behind  16.3 us
    ppermute x4, starting transfers between devices, shifted_2(): lax.ppermute(value, axis, [(i, (i + by) % length) for i in range(length)])  12.1 us
    ppermute x4, waiting for transfers between devices, shifted_2(): lax.ppermute(value, axis, [(i, (i + by) % length) for i in range(length)])  10.5 us
    slice x4, local copies, waits for them, and re-layouts, extended(): lax.slice_in_dim(cells, cells.shape[dim] - width, cells.shape[dim], axis=...  10.2 us
    ppermute x3, starting transfers between devices, extended(): lax.ppermute(tail, axis, [(i, (i + 1) % count) for i in range(ends)])  7.9 us
    add x9, local copies, waits for them, and re-layouts, interpolate(): jnp.where(left_hit, 1.0 - weight, 0.0) + jnp.where(right_hit, weight, 0.0)  7.58 us
    unnamed x12, other arithmetic  7.08 us
    ppermute x3, starting transfers between devices, extended(): lax.ppermute(head, axis, [((i + 1) % count, i) for i in range(ends)])  6.96 us
  transfers between devices with their start and end apart: 12, of which 3 were waited for; matrix products, arithmetic and copies ran while one was open for 26% of the time, Pallas kernels for 0%

commit v1 on v0

v1 whole, which is shorter than its diff:
```python
import jax
import jax.numpy as jnp
from jax import lax
from jax.experimental import pallas as pl
from jax.experimental.pallas import tpu as pltpu
from jax.sharding import PartitionSpec as P

MESH = pl.DeviceIdType.MESH
pair_list = ((0, 0), (1, 1), (2, 2), (0, 1), (0, 2), (1, 2))
CA, CR, CX = 8, 64, 128
NCH = 21
LINES = CA * CR
CAP = LINES // 4
GROUPS = CR // 8
f32 = jnp.float32
VMEM_LIMIT = 48000 * 2**10


def strain_norm(s):
    normal = s[0] * s[0] + s[1] * s[1] + s[2] * s[2]
    shearing = s[3] * s[3] + s[4] * s[4] + s[5] * s[5]
    return jnp.sqrt(2.0 * normal + 4.0 * shearing)


def products(raw):
    vel, strain = raw[:3], raw[3:]
    magnitude = strain_norm(strain)
    fields = list(vel)
    fields += [vel[i] * vel[j] for i, j in pair_list]
    fields += strain
    fields += [magnitude * s for s in strain]
    return fields, magnitude


def contract(filtered):
    strain = [filtered[9 + c] for c in range(6)]
    four_norm = 4.0 * strain_norm(strain)
    sums = []
    for channels in ((0, 1, 2), (3, 4, 5)):
        lm = mm = None
        for c in channels:
            i, j = pair_list[c]
            leonard = filtered[3 + c] - filtered[i] * filtered[j]
            model = filtered[15 + c] - four_norm * strain[c]
            lm = leonard * model if lm is None else lm + leonard * model
            mm = model * model if mm is None else mm + model * model
        sums.append((lm, mm))
    (lm_a, mm_a), (lm_b, mm_b) = sums
    return 0.5 * lm_a + lm_b, 0.25 * mm_a + 0.5 * mm_b


def exchange_kernel(
    vel, strain, lm_avg, mm_avg, owner, block, offset, frac, count,
    lines, lm_here, mm_here, mag, columns_out,
    raw, cols, col_send, halo_prod, ax_done, az_done, row_send, row_recv, rad_done,
    own, table, reply, ask, asked_vm, asked_sm, place_vm, place_sm,
    owner_v, block_v, offset_v, frac_v, count_s, stack,
    load_sem, send_sem, recv_sem,
):
    az, rad, ax = lax.axis_index("az"), lax.axis_index("rad"), lax.axis_index("ax")
    n_az, n_rad, n_ax = lax.axis_size("az"), lax.axis_size("rad"), lax.axis_size("ax")
    up = (lax.rem(az + 1, n_az), rad, ax)
    down = (lax.rem(az + n_az - 1, n_az), rad, ax)
    partner = (az, 1 - rad, ax)
    fore = (az, rad, lax.rem(ax + 1, n_ax))
    aft = (az, rad, lax.rem(ax + n_ax - 1, n_ax))

    barrier = pltpu.get_barrier_semaphore()
    for target in (up, down, partner, fore, aft):
        pl.semaphore_signal(barrier, inc=1, device_id=target, device_id_type=MESH)

    loads = []

    def load(src, dst):
        copy = pltpu.make_async_copy(src, dst, load_sem.at[len(loads)])
        copy.start()
        loads.append(copy)
        return copy

    small = [load(owner, owner_v), load(block, block_v), load(offset, offset_v), load(frac, frac_v), load(count, count_s)]
    bulk = [load(vel, raw.at[0:3, 1 : CA + 1]), load(strain, raw.at[3:9, 1 : CA + 1])]
    tables = [load(lm_avg, own.at[0]), load(mm_avg, own.at[1])]
    later = [load(lm_avg, table.at[0, 0:LINES]), load(mm_avg, table.at[1, 0:LINES])]

    sent = []

    def send(src, dst, target):
        copy = pltpu.make_async_remote_copy(
            src_ref=src, dst_ref=dst, send_sem=send_sem.at[len(sent)], recv_sem=recv_sem.at[len(sent)],
            device_id=target, device_id_type=MESH,
        )
        copy.start()
        sent.append(copy)
        return copy

    for copy in small:
        copy.wait()
    own_id = owner_v[:, 0, :]
    wanted = block_v[:, 0, :]
    self_id = (az * n_rad + rad) * n_ax + ax
    down_id = (down[0] * n_rad + rad) * n_ax + ax
    up_id = (up[0] * n_rad + rad) * n_ax + ax
    rad_id = (az * n_rad + 1 - rad) * n_ax + ax
    line_no = lax.broadcasted_iota(jnp.int32, (CA, CR), 0) * CR + lax.broadcasted_iota(jnp.int32, (CA, CR), 1)
    live = line_no < count_s[self_id]
    hits = [live & (own_id == peer) for peer in (down_id, up_id, rad_id)]
    masks = jnp.concatenate([jnp.where(h, 1.0, 0.0) for h in hits], axis=0)
    row = lax.broadcasted_iota(jnp.int32, (CR, CR), 0)
    col = lax.broadcasted_iota(jnp.int32, (CR, CR), 1)
    prefix = jnp.dot(masks, jnp.where(row <= col, 1.0, 0.0), preferred_element_type=f32)
    totals = jnp.dot(masks, jnp.ones((CR, CR), f32), preferred_element_type=f32)
    row3 = lax.broadcasted_iota(jnp.int32, (3 * CA, 3 * CA), 0)
    col3 = lax.broadcasted_iota(jnp.int32, (3 * CA, 3 * CA), 1)
    before = jnp.where((row3 > col3) & (row3 // CA == col3 // CA), 1.0, 0.0)
    rank = (prefix + jnp.dot(before, totals, preferred_element_type=f32)).astype(jnp.int32) - 1
    slot = jnp.full((CA, CR), -1, jnp.int32)
    place = jnp.where(live, wanted, line_no)
    for k in range(3):
        here = rank[k * CA : (k + 1) * CA] + k * CAP
        slot = jnp.where(hits[k], here, slot)
        place = jnp.where(hits[k], here + LINES, place)
    place_vm[:, 0:CR] = place
    stack[...] = jnp.zeros((CX, CX), f32)
    stack[0:CA, 0:CR] = slot.astype(f32)
    stack[CA : 2 * CA, 0:CR] = wanted.astype(f32)
    stack[2 * CA : 3 * CA, 0:CR] = offset_v[:, 0, :].astype(f32)
    stack[3 * CA : 4 * CA, 0:CR] = frac_v[:, 0, :]
    turned = jnp.transpose(stack[...])[0:CR]
    columns_out[...] = turned
    slots = lax.broadcasted_iota(jnp.int32, (CR, CX), 1).astype(f32)
    found = [jnp.zeros((CR, CX), f32)] * 3
    for a in range(CA):
        at = jnp.broadcast_to(turned[:, a : a + 1], (CR, CX)) - slots
        number = jnp.broadcast_to(turned[:, CA + a : CA + a + 1], (CR, CX))
        for k in range(3):
            found[k] = jnp.where(at == float(k * CAP), number, found[k])
    for k in range(3):
        ask[k] = jnp.broadcast_to(jnp.sum(found[k], axis=0, keepdims=True), (8, CX)).astype(jnp.int32)
    to_place = pltpu.make_async_copy(place_vm, place_sm, load_sem.at[len(loads)])
    to_place.start()

    pl.semaphore_wait(barrier, 5)

    queries = [send(ask.at[0], asked_vm.at[0], down), send(ask.at[1], asked_vm.at[1], up), send(ask.at[2], asked_vm.at[2], partner)]
    halos = [
        send(strain.at[:, CA - 1], raw.at[3:9, 0], up),
        send(strain.at[:, 0], raw.at[3:9, CA + 1], down),
        send(vel.at[:, CA - 1], raw.at[0:3, 0], up),
        send(vel.at[:, 0], raw.at[0:3, CA + 1], down),
    ]

    lane = lax.broadcasted_iota(jnp.int32, (8, CX), 1)
    for copy in bulk:
        copy.wait()

    @pl.loop(0, CA)
    def pack(a):
        first = last = jnp.zeros((8, CX), f32)
        for g in range(GROUPS):
            for c in range(9):
                at = 9 * g + c
                moved = raw[c, a + 1, 8 * g : 8 * g + 8]
                moved = pltpu.roll(moved, at, 1) if at else moved
                first = jnp.where(lane == at, moved, first)
                last = jnp.where(lane == (at - 1) % CX, moved, last)
        col_send[0, a] = first
        col_send[1, a] = last

    sides = [send(col_send.at[0], cols.at[1, 1 : CA + 1], aft), send(col_send.at[1], cols.at[0, 1 : CA + 1], fore)]

    for copy in queries:
        copy.wait()
    to_asked = pltpu.make_async_copy(asked_vm, asked_sm, load_sem.at[len(loads) + 1])
    to_asked.start()
    for copy in tables:
        copy.wait()
    to_asked.wait()
    for copy in sides:
        copy.wait()
    corners = [
        send(cols.at[:, CA], cols.at[:, 0], up),
        send(cols.at[:, 1], cols.at[:, CA + 1], down),
    ]

    @pl.loop(0, 3 * (CAP // 8))
    def answer(step):
        k = step // (CAP // 8)
        base = (step % (CAP // 8)) * 8
        for j in range(8):
            number = jnp.clip(asked_sm[k, 0, base + j], 0, LINES - 1)
            for ch in range(2):
                reply[k, ch, pl.ds(base + j, 1)] = own[ch, pl.ds(number, 1)]

    replies = [
        send(reply.at[0], table.at[:, LINES : LINES + CAP], up),
        send(reply.at[1], table.at[:, LINES + CAP : LINES + 2 * CAP], down),
        send(reply.at[2], table.at[:, LINES + 2 * CAP : LINES + 3 * CAP], partner),
    ]

    keep_aft = jnp.where(ax > 0, 1.0, 0.0)
    keep_fore = jnp.where(ax < n_ax - 1, 1.0, 0.0)
    aft_lane = lax.rem(lane, 9) == 0

    def axial(l, ours):
        low, high = cols[0, l] * keep_aft, cols[1, l] * keep_fore
        ends = []
        for c in range(9):
            low_c = pltpu.roll(low, (1 - c) % CX, 1) if c != 1 else low
            high_c = pltpu.roll(high, CX - 1 - c, 1)
            ends.append(jnp.where(aft_lane, low_c, high_c))
        ends, _ = products(ends)
        for ch in range(NCH):
            halo_prod[ch] = ends[ch]
        for g in range(GROUPS):
            rows = slice(8 * g, 8 * g + 8)
            fields, norm = products([raw[c, l, rows] for c in range(9)])
            if ours:
                mag[l - 1, rows] = norm
            for ch in range(NCH):
                value = fields[ch]
                end = halo_prod[ch]
                end = pltpu.roll(end, CX - 9 * g, 1) if g else end
                left = jnp.where(lane == 0, end, pltpu.roll(value, 1, 1))
                right = jnp.where(lane == CX - 1, end, pltpu.roll(value, CX - 1, 1))
                ax_done[ch, l, rows] = (value + value) + (left + right)

    def azimuthal(ch, layers):
        edges = {}
        for g in range(GROUPS):
            rows = slice(8 * g, 8 * g + 8)
            value = {}
            for l in layers:
                for n in (l - 1, l, l + 1):
                    if n not in value:
                        value[n] = ax_done[ch, n, rows]
                out = (value[l] + value[l]) + (value[l - 1] + value[l + 1])
                az_done[ch, l - 1, rows] = out
                if g == 0:
                    edges[l] = out[0:1]
                if g == GROUPS - 1:
                    row_send[l - 1, pl.ds(ch, 1)] = jnp.where(rad == 0, out[7:8], edges[l])

    sub = lax.broadcasted_iota(jnp.int32, (CR, CX), 0)

    def radial(a):
        for ch in range(NCH):
            value = az_done[ch, a]
            halo = row_recv[a, ch : ch + 1]
            above = jnp.where(rad == 1, halo, 0.0)
            below = jnp.where(rad == 0, halo, 0.0)
            prior = jnp.where(sub == 0, above, pltpu.roll(value, 1, 0))
            after = jnp.where(sub == CR - 1, below, pltpu.roll(value, CR - 1, 0))
            rad_done[ch] = ((value + value) + (prior + after)) * (1.0 / 64.0)
        for g in range(GROUPS):
            rows = slice(8 * g, 8 * g + 8)
            lm, mm = contract([rad_done[ch, rows] for ch in range(NCH)])
            lm_here[a, rows] = lm
            mm_here[a, rows] = mm

    pl.loop(1, CA + 1)(lambda l: axial(l, True))
    inner = tuple(range(2, CA))
    pl.loop(0, NCH)(lambda ch: azimuthal(ch, inner))
    rows_in = [send(row_send.at[1 : CA - 1], row_recv.at[1 : CA - 1], partner)]
    rows_in[0].wait()
    pl.loop(1, CA - 1)(radial)

    for copy in halos + corners:
        copy.wait()
    pl.loop(0, 2)(lambda i: axial(i * (CA + 1), False))

    pl.loop(0, NCH)(lambda ch: azimuthal(ch, (1, CA)))
    rows_out = [send(row_send.at[0], row_recv.at[0], partner), send(row_send.at[CA - 1], row_recv.at[CA - 1], partner)]
    for copy in rows_out:
        copy.wait()

    @pl.loop(0, 2)
    def edge_radial(i):
        radial(i * (CA - 1))

    for copy in later + replies:
        copy.wait()
    to_place.wait()

    @pl.loop(0, LINES // 8)
    def put(step):
        a = step // GROUPS
        base = (step % GROUPS) * 8
        for j in range(8):
            number = jnp.clip(place_sm[a, base + j], 0, LINES + 3 * CAP - 1)
            for ch in range(2):
                lines[ch, pl.ds(step * 8 + j, 1)] = table[ch, pl.ds(number, 1)]


def relax_kernel(lines, lm_here, mm_here, mag, columns, lm_new, mm_new, eddy):
    cell = lax.broadcasted_iota(jnp.int32, (CR, CX), 1)
    for a in range(CA):
        shift = jnp.broadcast_to(columns[:, 2 * CA + a : 2 * CA + a + 1], (CR, CX)).astype(jnp.int32)
        weight = jnp.broadcast_to(columns[:, 3 * CA + a : 3 * CA + a + 1], (CR, CX))
        anchor = cell - shift
        left = jnp.maximum(anchor, 0)
        right = jnp.clip(anchor + 1, 0, CX - 1)
        upstream = []
        for ch in range(2):
            line = lines[ch, a * CR : (a + 1) * CR]
            upstream.append(
                (1.0 - weight) * jnp.take_along_axis(line, left, axis=1)
                + weight * jnp.take_along_axis(line, right, axis=1)
            )
        up_lm, up_mm = upstream
        theta = 0.5 * jnp.sqrt(jnp.sqrt(jnp.sqrt(jnp.maximum(up_lm, 0.0) * up_mm)))
        eps = theta / (1.0 + theta)
        lm = jnp.maximum(eps * lm_here[a] + (1.0 - eps) * up_lm, 0.0)
        mm = eps * mm_here[a] + (1.0 - eps) * up_mm
        lm_new[a] = lm
        mm_new[a] = mm
        eddy[a] = 0.25 * lm / mm * mag[a]


def on_device(velocity, strain_rate, lm_average, mm_average, source_owner, source_block, offset_cells, fraction, query_count):
    grid = (CA, CR, CX)
    line_form = (LINES, CX)
    flat = (CA, 1, CR)
    SDS = jax.ShapeDtypeStruct
    VMEM = pltpu.VMEM
    whole = pl.BlockSpec(memory_space=pltpu.VMEM)
    lines, lm_here, mm_here, mag, columns = pl.pallas_call(
        exchange_kernel,
        out_shape=[VMEM((2,) + line_form, f32), VMEM(grid, f32), VMEM(grid, f32), VMEM(grid, f32), VMEM((CR, CX), f32)],
        in_specs=[pl.BlockSpec(memory_space=pltpu.HBM)] * 9,
        out_specs=[whole] * 5,
        scratch_shapes=[
            VMEM((9, CA + 2, CR, CX), f32),
            VMEM((2, CA + 2, 8, CX), f32),
            VMEM((2, CA, 8, CX), f32),
            VMEM((NCH, 8, CX), f32),
            VMEM((NCH, CA + 2, CR, CX), f32),
            VMEM((NCH, CA, CR, CX), f32),
            VMEM((CA, 24, CX), f32),
            VMEM((CA, 24, CX), f32),
            VMEM((NCH, CR, CX), f32),
            VMEM((2,) + line_form, f32),
            VMEM((2, LINES + 3 * CAP, CX), f32),
            VMEM((3, 2, CAP, CX), f32),
            VMEM((3, 8, CX), jnp.int32),
            VMEM((3, 8, CX), jnp.int32),
            pltpu.SMEM((3, 8, CX), jnp.int32),
            VMEM((CA, CX), jnp.int32),
            pltpu.SMEM((CA, CX), jnp.int32),
            VMEM(flat, jnp.int32),
            VMEM(flat, jnp.int32),
            VMEM(flat, jnp.int32),
            VMEM(flat, f32),
            pltpu.SMEM(query_count.shape, jnp.int32),
            VMEM((CX, CX), f32),
            pltpu.SemaphoreType.DMA((16,)),
            pltpu.SemaphoreType.DMA((20,)),
            pltpu.SemaphoreType.DMA((20,)),
        ],
        compiler_params=pltpu.CompilerParams(collective_id=0, has_side_effects=True, vmem_limit_bytes=VMEM_LIMIT),
        name="exchange",
    )(*(pltpu.with_memory_space_constraint(x, pltpu.HBM) for x in (
        velocity, strain_rate, lm_average.reshape(line_form), mm_average.reshape(line_form),
        source_owner.reshape(flat), source_block.reshape(flat), offset_cells.reshape(flat), fraction.reshape(flat),
        query_count,
    )))
    return pl.pallas_call(
        relax_kernel,
        out_shape=[SDS(grid, f32)] * 3,
        in_specs=[whole] * 5,
        out_specs=[whole] * 3,
        compiler_params=pltpu.CompilerParams(vmem_limit_bytes=32 * 2**20),
        name="relax",
    )(lines, lm_here, mm_here, mag, columns)


def solution(mesh):
    cells, lines = P(None, "az", "rad", "ax"), P("az", "rad", "ax")
    return jax.shard_map(
        on_device,
        mesh=mesh,
        in_specs=(cells, cells) + (lines,) * 6 + (P(),),
        out_specs=(lines, lines, lines),
        check_vma=False,
    )
```

time: 117 us -> 42.3 us (0.36)
  the two profiles are of different devices: /device:TPU:103 before, /device:TPU:1 now
where the time goes in v1:
time: 42.3 us; the launch traced here: 42.2 us
  Pallas kernels  41.6 us (98%)
  between operations  0.64 us (2%)
    pallas_call x1, Pallas kernels, on_device(): pl.pallas_call(exchange_kernel, out_shape=[VMEM((2,) + line_form, f32), V...  39.4 us
    pallas_call x1, Pallas kernels, on_device(): pl.pallas_call(relax_kernel, out_shape=[SDS(grid, f32)] * 3, in_specs=[wh...  2.22 us

profile of v1, /device:TPU:1, one launch (start us, length us, event | category | flops | bytes accessed | tf_op | source)
XLA Modules:
  0.0 42.2 jit_solution(6933644732103164335)
XLA Ops:
  0.6 39.4 %exchange.1 = (f32[2,512,128]{2,1,0:T(8,128)S(1)}, f32[8,64,128]{2,1,0:T(8,128)S(1)}, f32[8,64,128]{2,1,0:T(8,128)S(1)}, f32[8,64,128]{2,1,0:T(8,128)S(1)}, f32[64,128]{1,0:T(8,128)S(1)}) custom-call(f32[3,8,64,128]{3,2,1,0:T(8,128)} %vel.1, f32[6,8,64,128]{3,2,1,0:T(8,128)} %strain.1, f32[512,128]{1,0:T(8,128)} %bitcast.6, f32[512,128]{1,0:T(8,128)} %bitcast.7, ...), custom_call_target="tpu_custom_call" | custom-call | tf_op jit(solution)/shard_map/exchange/pallas_call | solution.py:326
  40.0 2.2 %relax.1 = (f32[8,64,128]{2,1,0:T(8,128)}, f32[8,64,128]{2,1,0:T(8,128)}, f32[8,64,128]{2,1,0:T(8,128)}) custom-call(f32[2,512,128]{2,1,0:T(8,128)S(1)} %get-tuple-element.8.lines, f32[8,64,128]{2,1,0:T(8,128)S(1)} %get-tuple-element.9.lm_here, f32[8,64,128]{2,1,0:T(8,128)S(1)} %get-tuple-element.10.mm_here, f32[8,64,128]{2,1,0:T(8,128)S(1)} %get-tuple-element.11.mag, ...), custom_call_target="tpu_custom_call" | custom-call | tf_op jit(solution)/shard_map/relax/pallas_call | solution.py:366

commit v2 on v1

--- a/solution.py
+++ b/solution.py
@@ -93,6 +93,7 @@
         sent.append(copy)
         return copy
 
+    lane = lax.broadcasted_iota(jnp.int32, (8, CX), 1)
     for copy in small:
         copy.wait()
     own_id = owner_v[:, 0, :]
@@ -139,17 +140,7 @@
     to_place = pltpu.make_async_copy(place_vm, place_sm, load_sem.at[len(loads)])
     to_place.start()
 
-    pl.semaphore_wait(barrier, 5)
-
-    queries = [send(ask.at[0], asked_vm.at[0], down), send(ask.at[1], asked_vm.at[1], up), send(ask.at[2], asked_vm.at[2], partner)]
-    halos = [
-        send(strain.at[:, CA - 1], raw.at[3:9, 0], up),
-        send(strain.at[:, 0], raw.at[3:9, CA + 1], down),
-        send(vel.at[:, CA - 1], raw.at[0:3, 0], up),
-        send(vel.at[:, 0], raw.at[0:3, CA + 1], down),
-    ]
-
-    lane = lax.broadcasted_iota(jnp.int32, (8, CX), 1)
+
     for copy in bulk:
         copy.wait()
 
@@ -166,7 +157,25 @@
         col_send[0, a] = first
         col_send[1, a] = last
 
-    sides = [send(col_send.at[0], cols.at[1, 1 : CA + 1], aft), send(col_send.at[1], cols.at[0, 1 : CA + 1], fore)]
+    pl.semaphore_wait(barrier, 5)
+
+    queries = [
+        send(ask.at[0], asked_vm.at[0], down),
+        send(ask.at[1], asked_vm.at[1], up),
+        send(ask.at[2], asked_vm.at[2], partner),
+    ]
+    sides = [
+        send(col_send.at[0], cols.at[1, 1 : CA + 1], aft),
+        send(col_send.at[1], cols.at[0, 1 : CA + 1], fore),
+    ]
+    halos = [
+        send(vel.at[:, CA - 1], raw.at[0:3, 0], up),
+        send(vel.at[:, 0], raw.at[0:3, CA + 1], down),
+    ]
+    halos += [
+        send(strain.at[:, CA - 1], raw.at[3:9, 0], up),
+        send(strain.at[:, 0], raw.at[3:9, CA + 1], down),
+    ]
 
     for copy in queries:
         copy.wait()
@@ -175,22 +184,22 @@
     for copy in tables:
         copy.wait()
     to_asked.wait()
+
+    @pl.loop(0, 3 * (CAP // 64))
+    def answer(step):
+        k = step // (CAP // 64)
+        base = (step % (CAP // 64)) * 64
+        for j in range(64):
+            number = jnp.clip(asked_sm[k, 0, base + j], 0, LINES - 1)
+            for ch in range(2):
+                reply[k, ch, pl.ds(base + j, 1)] = own[ch, pl.ds(number, 1)]
+
     for copy in sides:
         copy.wait()
     corners = [
         send(cols.at[:, CA], cols.at[:, 0], up),
         send(cols.at[:, 1], cols.at[:, CA + 1], down),
     ]
-
-    @pl.loop(0, 3 * (CAP // 8))
-    def answer(step):
-        k = step // (CAP // 8)
-        base = (step % (CAP // 8)) * 8
-        for j in range(8):
-            number = jnp.clip(asked_sm[k, 0, base + j], 0, LINES - 1)
-            for ch in range(2):
-                reply[k, ch, pl.ds(base + j, 1)] = own[ch, pl.ds(number, 1)]
-
     replies = [
         send(reply.at[0], table.at[:, LINES : LINES + CAP], up),
         send(reply.at[1], table.at[:, LINES + CAP : LINES + 2 * CAP], down),
@@ -270,26 +279,26 @@
 
     pl.loop(0, NCH)(lambda ch: azimuthal(ch, (1, CA)))
     rows_out = [send(row_send.at[0], row_recv.at[0], partner), send(row_send.at[CA - 1], row_recv.at[CA - 1], partner)]
+    for copy in later + replies:
+        copy.wait()
+    to_place.wait()
+
+    @pl.loop(0, LINES // 64)
+    def put(step):
+        a = step // (CR // 64)
+        base = (step % (CR // 64)) * 64
+        for j in range(64):
+            number = jnp.clip(place_sm[a, base + j], 0, LINES + 3 * CAP - 1)
+            for ch in range(2):
+                lines[ch, pl.ds(step * 64 + j, 1)] = table[ch, pl.ds(number, 1)]
+
+
     for copy in rows_out:
         copy.wait()
 
     @pl.loop(0, 2)
     def edge_radial(i):
         radial(i * (CA - 1))
-
-    for copy in later + replies:
-        copy.wait()
-    to_place.wait()
-
-    @pl.loop(0, LINES // 8)
-    def put(step):
-        a = step // GROUPS
-        base = (step % GROUPS) * 8
-        for j in range(8):
-            number = jnp.clip(place_sm[a, base + j], 0, LINES + 3 * CAP - 1)
-            for ch in range(2):
-                lines[ch, pl.ds(step * 8 + j, 1)] = table[ch, pl.ds(number, 1)]
-
 
 def relax_kernel(lines, lm_here, mm_here, mag, columns, lm_new, mm_new, eddy):
     cell = lax.broadcasted_iota(jnp.int32, (CR, CX), 1)

time: 42.3 us -> 34.7 us (0.82)
  Pallas kernels: 41.6 us -> 34 us
    pallas_call x1, Pallas kernels: 39.4 us -> 31.8 us  [on_device(): pl.pallas_call(exchange_kernel, out_shape=[VMEM((2,) + line_form, f32), V...]
where the time goes in v2:
time: 34.7 us; the launch traced here: 34.6 us
  Pallas kernels  34 us (98%)
  between operations  0.64 us (2%)
    pallas_call x1, Pallas kernels, on_device(): pl.pallas_call(exchange_kernel, out_shape=[VMEM((2,) + line_form, f32), V...  31.8 us
    pallas_call x1, Pallas kernels, on_device(): pl.pallas_call(relax_kernel, out_shape=[SDS(grid, f32)] * 3, in_specs=[wh...  2.22 us

profile of v2, /device:TPU:1, one launch (start us, length us, event | category | flops | bytes accessed | tf_op | source)
XLA Modules:
  0.0 34.6 jit_solution(9326366592625154871)
XLA Ops:
  0.6 31.8 %exchange.1 = (f32[2,512,128]{2,1,0:T(8,128)S(1)}, f32[8,64,128]{2,1,0:T(8,128)S(1)}, f32[8,64,128]{2,1,0:T(8,128)S(1)}, f32[8,64,128]{2,1,0:T(8,128)S(1)}, f32[64,128]{1,0:T(8,128)S(1)}) custom-call(f32[3,8,64,128]{3,2,1,0:T(8,128)} %vel.1, f32[6,8,64,128]{3,2,1,0:T(8,128)} %strain.1, f32[512,128]{1,0:T(8,128)} %bitcast.6, f32[512,128]{1,0:T(8,128)} %bitcast.7, ...), custom_call_target="tpu_custom_call" | custom-call | tf_op jit(solution)/shard_map/exchange/pallas_call | solution.py:335
  32.4 2.2 %relax.1 = (f32[8,64,128]{2,1,0:T(8,128)}, f32[8,64,128]{2,1,0:T(8,128)}, f32[8,64,128]{2,1,0:T(8,128)}) custom-call(f32[2,512,128]{2,1,0:T(8,128)S(1)} %get-tuple-element.8.lines, f32[8,64,128]{2,1,0:T(8,128)S(1)} %get-tuple-element.9.lm_here, f32[8,64,128]{2,1,0:T(8,128)S(1)} %get-tuple-element.10.mm_here, f32[8,64,128]{2,1,0:T(8,128)S(1)} %get-tuple-element.11.mag, ...), custom_call_target="tpu_custom_call" | custom-call | tf_op jit(solution)/shard_map/relax/pallas_call | solution.py:375

commit v3 on v2

--- a/solution.py
+++ b/solution.py
@@ -52,7 +52,7 @@
 def exchange_kernel(
     vel, strain, lm_avg, mm_avg, owner, block, offset, frac, count,
     lines, lm_here, mm_here, mag, columns_out,
-    raw, cols, col_send, halo_prod, ax_done, az_done, row_send, row_recv, rad_done,
+    raw, cols, col_send, ax_done, az_done, row_send, row_recv, rad_done,
     own, table, reply, ask, asked_vm, asked_sm, place_vm, place_sm,
     owner_v, block_v, offset_v, frac_v, count_s, stack,
     load_sem, send_sem, recv_sem,
@@ -93,6 +93,7 @@
         sent.append(copy)
         return copy
 
+    halos = []
     lane = lax.broadcasted_iota(jnp.int32, (8, CX), 1)
     for copy in small:
         copy.wait()
@@ -168,7 +169,7 @@
         send(col_send.at[0], cols.at[1, 1 : CA + 1], aft),
         send(col_send.at[1], cols.at[0, 1 : CA + 1], fore),
     ]
-    halos = [
+    halos += [
         send(vel.at[:, CA - 1], raw.at[0:3, 0], up),
         send(vel.at[:, 0], raw.at[0:3, CA + 1], down),
     ]
@@ -217,21 +218,21 @@
             low_c = pltpu.roll(low, (1 - c) % CX, 1) if c != 1 else low
             high_c = pltpu.roll(high, CX - 1 - c, 1)
             ends.append(jnp.where(aft_lane, low_c, high_c))
-        ends, _ = products(ends)
-        for ch in range(NCH):
-            halo_prod[ch] = ends[ch]
         for g in range(GROUPS):
             rows = slice(8 * g, 8 * g + 8)
-            fields, norm = products([raw[c, l, rows] for c in range(9)])
+            here, behind, ahead = [], [], []
+            for c in range(9):
+                value = raw[c, l, rows]
+                end = pltpu.roll(ends[c], CX - 9 * g, 1) if g else ends[c]
+                here.append(value)
+                behind.append(jnp.where(lane == 0, end, pltpu.roll(value, 1, 1)))
+                ahead.append(jnp.where(lane == CX - 1, end, pltpu.roll(value, CX - 1, 1)))
+            here, norm = products(here)
+            behind, ahead = products(behind)[0], products(ahead)[0]
             if ours:
                 mag[l - 1, rows] = norm
             for ch in range(NCH):
-                value = fields[ch]
-                end = halo_prod[ch]
-                end = pltpu.roll(end, CX - 9 * g, 1) if g else end
-                left = jnp.where(lane == 0, end, pltpu.roll(value, 1, 1))
-                right = jnp.where(lane == CX - 1, end, pltpu.roll(value, CX - 1, 1))
-                ax_done[ch, l, rows] = (value + value) + (left + right)
+                ax_done[ch, l, rows] = (here[ch] + here[ch]) + (behind[ch] + ahead[ch])
 
     def azimuthal(ch, layers):
         edges = {}
@@ -243,22 +244,22 @@
                     if n not in value:
                         value[n] = ax_done[ch, n, rows]
                 out = (value[l] + value[l]) + (value[l - 1] + value[l + 1])
-                az_done[ch, l - 1, rows] = out
+                az_done[ch, l - 1, 8 * g + 8 : 8 * g + 16] = out
                 if g == 0:
                     edges[l] = out[0:1]
                 if g == GROUPS - 1:
                     row_send[l - 1, pl.ds(ch, 1)] = jnp.where(rad == 0, out[7:8], edges[l])
 
-    sub = lax.broadcasted_iota(jnp.int32, (CR, CX), 0)
-
     def radial(a):
         for ch in range(NCH):
-            value = az_done[ch, a]
+            value = az_done[ch, a, 8 : CR + 8]
             halo = row_recv[a, ch : ch + 1]
             above = jnp.where(rad == 1, halo, 0.0)
             below = jnp.where(rad == 0, halo, 0.0)
-            prior = jnp.where(sub == 0, above, pltpu.roll(value, 1, 0))
-            after = jnp.where(sub == CR - 1, below, pltpu.roll(value, CR - 1, 0))
+            az_done[ch, a, 7:8] = above
+            az_done[ch, a, CR + 8 : CR + 9] = below
+            prior = az_done[ch, a, 7 : CR + 7]
+            after = az_done[ch, a, 9 : CR + 9]
             rad_done[ch] = ((value + value) + (prior + after)) * (1.0 / 64.0)
         for g in range(GROUPS):
             rows = slice(8 * g, 8 * g + 8)
@@ -341,9 +342,8 @@
             VMEM((9, CA + 2, CR, CX), f32),
             VMEM((2, CA + 2, 8, CX), f32),
             VMEM((2, CA, 8, CX), f32),
-            VMEM((NCH, 8, CX), f32),
             VMEM((NCH, CA + 2, CR, CX), f32),
-            VMEM((NCH, CA, CR, CX), f32),
+            VMEM((NCH, CA, CR + 16, CX), f32),
             VMEM((CA, 24, CX), f32),
             VMEM((CA, 24, CX), f32),
             VMEM((NCH, CR, CX), f32),

time: 34.7 us -> 33.1 us (0.954)
  Pallas kernels: 34 us -> 32.3 us
    pallas_call x1, Pallas kernels: 31.8 us -> 30.1 us  [on_device(): pl.pallas_call(exchange_kernel, out_shape=[VMEM((2,) + line_form, f32), V...]
where the time goes in v3:
time: 33.1 us; the launch traced here: 33 us
  Pallas kernels  32.3 us (98%)
  between operations  0.64 us (2%)
    pallas_call x1, Pallas kernels, on_device(): pl.pallas_call(exchange_kernel, out_shape=[VMEM((2,) + line_form, f32), V...  30.1 us
    pallas_call x1, Pallas kernels, on_device(): pl.pallas_call(relax_kernel, out_shape=[SDS(grid, f32)] * 3, in_specs=[wh...  2.22 us

profile of v3, /device:TPU:1, one launch (start us, length us, event | category | flops | bytes accessed | tf_op | source)
XLA Modules:
  0.0 33.0 jit_solution(10237442153087288032)
XLA Ops:
  0.6 30.1 %exchange.1 = (f32[2,512,128]{2,1,0:T(8,128)S(1)}, f32[8,64,128]{2,1,0:T(8,128)S(1)}, f32[8,64,128]{2,1,0:T(8,128)S(1)}, f32[8,64,128]{2,1,0:T(8,128)S(1)}, f32[64,128]{1,0:T(8,128)S(1)}) custom-call(f32[3,8,64,128]{3,2,1,0:T(8,128)} %vel.1, f32[6,8,64,128]{3,2,1,0:T(8,128)} %strain.1, f32[512,128]{1,0:T(8,128)} %bitcast.6, f32[512,128]{1,0:T(8,128)} %bitcast.7, ...), custom_call_target="tpu_custom_call" | custom-call | tf_op jit(solution)/shard_map/exchange/pallas_call | solution.py:336
  30.7 2.2 %relax.1 = (f32[8,64,128]{2,1,0:T(8,128)}, f32[8,64,128]{2,1,0:T(8,128)}, f32[8,64,128]{2,1,0:T(8,128)}) custom-call(f32[2,512,128]{2,1,0:T(8,128)S(1)} %get-tuple-element.8.lines, f32[8,64,128]{2,1,0:T(8,128)S(1)} %get-tuple-element.9.lm_here, f32[8,64,128]{2,1,0:T(8,128)S(1)} %get-tuple-element.10.mm_here, f32[8,64,128]{2,1,0:T(8,128)S(1)} %get-tuple-element.11.mag, ...), custom_call_target="tpu_custom_call" | custom-call | tf_op jit(solution)/shard_map/relax/pallas_call | solution.py:375

commit v4 on v3

--- a/solution.py
+++ b/solution.py
@@ -51,7 +51,8 @@
 
 def exchange_kernel(
     vel, strain, lm_avg, mm_avg, owner, block, offset, frac, count,
-    lines, lm_here, mm_here, mag, columns_out,
+    upstream, lm_here, mm_here, mag,
+    lines, columns,
     raw, cols, col_send, ax_done, az_done, row_send, row_recv, rad_done,
     own, table, reply, ask, asked_vm, asked_sm, place_vm, place_sm,
     owner_v, block_v, offset_v, frac_v, count_s, stack,
@@ -128,7 +129,7 @@
     stack[2 * CA : 3 * CA, 0:CR] = offset_v[:, 0, :].astype(f32)
     stack[3 * CA : 4 * CA, 0:CR] = frac_v[:, 0, :]
     turned = jnp.transpose(stack[...])[0:CR]
-    columns_out[...] = turned
+    columns[...] = turned
     slots = lax.broadcasted_iota(jnp.int32, (CR, CX), 1).astype(f32)
     found = [jnp.zeros((CR, CX), f32)] * 3
     for a in range(CA):
@@ -294,14 +295,6 @@
                 lines[ch, pl.ds(step * 64 + j, 1)] = table[ch, pl.ds(number, 1)]
 
 
-    for copy in rows_out:
-        copy.wait()
-
-    @pl.loop(0, 2)
-    def edge_radial(i):
-        radial(i * (CA - 1))
-
-def relax_kernel(lines, lm_here, mm_here, mag, columns, lm_new, mm_new, eddy):
     cell = lax.broadcasted_iota(jnp.int32, (CR, CX), 1)
     for a in range(CA):
         shift = jnp.broadcast_to(columns[:, 2 * CA + a : 2 * CA + a + 1], (CR, CX)).astype(jnp.int32)
@@ -309,18 +302,28 @@
         anchor = cell - shift
         left = jnp.maximum(anchor, 0)
         right = jnp.clip(anchor + 1, 0, CX - 1)
-        upstream = []
-        for ch in range(2):
-            line = lines[ch, a * CR : (a + 1) * CR]
-            upstream.append(
-                (1.0 - weight) * jnp.take_along_axis(line, left, axis=1)
-                + weight * jnp.take_along_axis(line, right, axis=1)
-            )
-        up_lm, up_mm = upstream
+        up_lm, up_mm = (
+            (1.0 - weight) * jnp.take_along_axis(line, left, axis=1) + weight * jnp.take_along_axis(line, right, axis=1)
+            for line in (lines[0, a * CR : (a + 1) * CR], lines[1, a * CR : (a + 1) * CR])
+        )
         theta = 0.5 * jnp.sqrt(jnp.sqrt(jnp.sqrt(jnp.maximum(up_lm, 0.0) * up_mm)))
         eps = theta / (1.0 + theta)
-        lm = jnp.maximum(eps * lm_here[a] + (1.0 - eps) * up_lm, 0.0)
-        mm = eps * mm_here[a] + (1.0 - eps) * up_mm
+        upstream[0, a] = eps
+        upstream[1, a] = (1.0 - eps) * up_lm
+        upstream[2, a] = (1.0 - eps) * up_mm
+
+    for copy in rows_out:
+        copy.wait()
+
+    @pl.loop(0, 2)
+    def edge_radial(i):
+        radial(i * (CA - 1))
+
+def relax_kernel(upstream, lm_here, mm_here, mag, lm_new, mm_new, eddy):
+    for a in range(CA):
+        eps = upstream[0, a]
+        lm = jnp.maximum(eps * lm_here[a] + upstream[1, a], 0.0)
+        mm = eps * mm_here[a] + upstream[2, a]
         lm_new[a] = lm
         mm_new[a] = mm
         eddy[a] = 0.25 * lm / mm * mag[a]
@@ -333,12 +336,14 @@
     SDS = jax.ShapeDtypeStruct
     VMEM = pltpu.VMEM
     whole = pl.BlockSpec(memory_space=pltpu.VMEM)
-    lines, lm_here, mm_here, mag, columns = pl.pallas_call(
+    upstream, lm_here, mm_here, mag = pl.pallas_call(
         exchange_kernel,
-        out_shape=[VMEM((2,) + line_form, f32), VMEM(grid, f32), VMEM(grid, f32), VMEM(grid, f32), VMEM((CR, CX), f32)],
+        out_shape=[VMEM((3,) + grid, f32), VMEM(grid, f32), VMEM(grid, f32), VMEM(grid, f32)],
         in_specs=[pl.BlockSpec(memory_space=pltpu.HBM)] * 9,
-        out_specs=[whole] * 5,
+        out_specs=[whole] * 4,
         scratch_shapes=[
+            VMEM((2,) + line_form, f32),
+            VMEM((CR, CX), f32),
             VMEM((9, CA + 2, CR, CX), f32),
             VMEM((2, CA + 2, 8, CX), f32),
             VMEM((2, CA, 8, CX), f32),
@@ -375,11 +380,11 @@
     return pl.pallas_call(
         relax_kernel,
         out_shape=[SDS(grid, f32)] * 3,
-        in_specs=[whole] * 5,
+        in_specs=[whole] * 4,
         out_specs=[whole] * 3,
         compiler_params=pltpu.CompilerParams(vmem_limit_bytes=32 * 2**20),
         name="relax",
-    )(lines, lm_here, mm_here, mag, columns)
+    )(upstream, lm_here, mm_here, mag)
 
 
 def solution(mesh):

time: 33.1 us -> 32.5 us (0.982)
  the two profiles are of different devices: /device:TPU:1 before, /device:TPU:192 now
where the time goes in v4:
time: 32.5 us; the launch traced here: 32.4 us
  Pallas kernels  31.7 us (98%)
  between operations  0.64 us (2%)
    pallas_call x1, Pallas kernels, on_device(): pl.pallas_call(exchange_kernel, out_shape=[VMEM((3,) + grid, f32), VMEM(g...  30.8 us
    pallas_call x1, Pallas kernels, on_device(): pl.pallas_call(relax_kernel, out_shape=[SDS(grid, f32)] * 3, in_specs=[wh...  0.95 us

profile of v4, /device:TPU:192, one launch (start us, length us, event | category | flops | bytes accessed | tf_op | source)
XLA Modules:
  0.0 32.4 jit_solution(14445944964764262391)
XLA Ops:
  0.6 30.8 %exchange.1 = (f32[3,8,64,128]{3,2,1,0:T(8,128)S(1)}, f32[8,64,128]{2,1,0:T(8,128)S(1)}, f32[8,64,128]{2,1,0:T(8,128)S(1)}, f32[8,64,128]{2,1,0:T(8,128)S(1)}) custom-call(f32[3,8,64,128]{3,2,1,0:T(8,128)} %vel.1, f32[6,8,64,128]{3,2,1,0:T(8,128)} %strain.1, f32[512,128]{1,0:T(8,128)} %bitcast.6, f32[512,128]{1,0:T(8,128)} %bitcast.7, s32[8,1,64]{2,1,0:T(1,128)} %bitcast.8, ...), custom_call_target="tpu_custom_call" | custom-call | tf_op jit(solution)/shard_map/exchange/pallas_call | solution.py:339
  31.4 1.0 %relax.1 = (f32[8,64,128]{2,1,0:T(8,128)}, f32[8,64,128]{2,1,0:T(8,128)}, f32[8,64,128]{2,1,0:T(8,128)}) custom-call(f32[3,8,64,128]{3,2,1,0:T(8,128)S(1)} %get-tuple-element.7.upstream, f32[8,64,128]{2,1,0:T(8,128)S(1)} %get-tuple-element.8.lm_here, f32[8,64,128]{2,1,0:T(8,128)S(1)} %get-tuple-element.9.mm_here, f32[8,64,128]{2,1,0:T(8,128)S(1)} %get-tuple-element.10.mag), custom_call_target="tpu_custom_call" | custom-call | tf_op jit(solution)/shard_map/relax/pallas_call | solution.py:380

commit v5 on v4

--- a/solution.py
+++ b/solution.py
@@ -187,26 +187,28 @@
         copy.wait()
     to_asked.wait()
 
-    @pl.loop(0, 3 * (CAP // 64))
-    def answer(step):
-        k = step // (CAP // 64)
-        base = (step % (CAP // 64)) * 64
-        for j in range(64):
-            number = jnp.clip(asked_sm[k, 0, base + j], 0, LINES - 1)
-            for ch in range(2):
-                reply[k, ch, pl.ds(base + j, 1)] = own[ch, pl.ds(number, 1)]
-
+    def answer(k):
+        @pl.loop(0, CAP // 64)
+        def lines_of(step):
+            base = step * 64
+            for j in range(64):
+                number = jnp.clip(asked_sm[k, 0, base + j], 0, LINES - 1)
+                for ch in range(2):
+                    reply[k, ch, pl.ds(base + j, 1)] = own[ch, pl.ds(number, 1)]
+
+    answer(0)
     for copy in sides:
         copy.wait()
     corners = [
         send(cols.at[:, CA], cols.at[:, 0], up),
         send(cols.at[:, 1], cols.at[:, CA + 1], down),
     ]
-    replies = [
-        send(reply.at[0], table.at[:, LINES : LINES + CAP], up),
-        send(reply.at[1], table.at[:, LINES + CAP : LINES + 2 * CAP], down),
-        send(reply.at[2], table.at[:, LINES + 2 * CAP : LINES + 3 * CAP], partner),
-    ]
+    replies = []
+    for k, target in enumerate((up, down, partner)):
+        if k:
+            answer(k)
+        first = LINES + k * CAP
+        replies.append(send(reply.at[k], table.at[:, first : first + CAP], target))
 
     keep_aft = jnp.where(ax > 0, 1.0, 0.0)
     keep_fore = jnp.where(ax < n_ax - 1, 1.0, 0.0)

time: 32.5 us -> 32.5 us (level)
  the two profiles are of different devices: /device:TPU:192 before, /device:TPU:1 now
where the time goes in v5:
time: 32.5 us; the launch traced here: 32.4 us
  Pallas kernels  31.7 us (98%)
  between operations  0.64 us (2%)
    pallas_call x1, Pallas kernels, on_device(): pl.pallas_call(exchange_kernel, out_shape=[VMEM((3,) + grid, f32), VMEM(g...  30.8 us
    pallas_call x1, Pallas kernels, on_device(): pl.pallas_call(relax_kernel, out_shape=[SDS(grid, f32)] * 3, in_specs=[wh...  0.95 us

profile of v5, /device:TPU:1, one launch (start us, length us, event | category | flops | bytes accessed | tf_op | source)
XLA Modules:
  0.0 32.4 jit_solution(2101060716704970036)
XLA Ops:
  0.6 30.8 %exchange.1 = (f32[3,8,64,128]{3,2,1,0:T(8,128)S(1)}, f32[8,64,128]{2,1,0:T(8,128)S(1)}, f32[8,64,128]{2,1,0:T(8,128)S(1)}, f32[8,64,128]{2,1,0:T(8,128)S(1)}) custom-call(f32[3,8,64,128]{3,2,1,0:T(8,128)} %vel.1, f32[6,8,64,128]{3,2,1,0:T(8,128)} %strain.1, f32[512,128]{1,0:T(8,128)} %bitcast.6, f32[512,128]{1,0:T(8,128)} %bitcast.7, s32[8,1,64]{2,1,0:T(1,128)} %bitcast.8, ...), custom_call_target="tpu_custom_call" | custom-call | tf_op jit(solution)/shard_map/exchange/pallas_call | solution.py:341
  31.4 1.0 %relax.1 = (f32[8,64,128]{2,1,0:T(8,128)}, f32[8,64,128]{2,1,0:T(8,128)}, f32[8,64,128]{2,1,0:T(8,128)}) custom-call(f32[3,8,64,128]{3,2,1,0:T(8,128)S(1)} %get-tuple-element.7.upstream, f32[8,64,128]{2,1,0:T(8,128)S(1)} %get-tuple-element.8.lm_here, f32[8,64,128]{2,1,0:T(8,128)S(1)} %get-tuple-element.9.mm_here, f32[8,64,128]{2,1,0:T(8,128)S(1)} %get-tuple-element.10.mag), custom_call_target="tpu_custom_call" | custom-call | tf_op jit(solution)/shard_map/relax/pallas_call | solution.py:382
